TPU v7x, 128 devices: a whole 4x4x4 slice. The times are simulated.
128 devices in a mesh: dp: 4 (over y), fsdp: 32 (over z, x, core).
Axes of the slice: x: 4, y: 4, z: 4, core: 2. Of those that a mesh axis runs over, the one named last changes fastest.
Arguments:
- block_input: bfloat16 [2, 16384, 1024], P(None, ('dp', 'fsdp')), may hold values from -6 to 6
- cotangent: bfloat16 [2, 16384, 1024], P(None, ('dp', 'fsdp')), may hold values from -6 to 6
- in_weight: float32 [1024, 3072], P('fsdp'), may hold values from -0.1875 to 0.1875
- out_weight: float32 [1024, 1024], P('fsdp'), may hold values from -0.1875 to 0.1875
- gate_weight: float32 [1024, 4608], P('fsdp'), may hold values from -0.1875 to 0.1875
- up_weight: float32 [1024, 4608], P('fsdp'), may hold values from -0.1875 to 0.1875
- down_weight: float32 [4608, 1024], P('fsdp'), may hold values from -0.09375 to 0.09375
- small_params: float32 [5, 1024], P(None, 'fsdp'), may hold values from 0.25 to 1.75
- in_first: float32 [1024, 3072], P('fsdp'), may hold values from -256 to 256
- out_first: float32 [1024, 1024], P('fsdp'), may hold values from -256 to 256
- gate_first: float32 [1024, 4608], P('fsdp'), may hold values from -32 to 32
- up_first: float32 [1024, 4608], P('fsdp'), may hold values from -32 to 32
- down_first: float32 [4608, 1024], P('fsdp'), may hold values from -80 to 80
- small_first: float32 [5, 1024], P(None, 'fsdp'), may hold values from -256 to 256
- in_second: float32 [1024, 3072], P('fsdp'), may hold values from 10485.76 to 41287.68
- out_second: float32 [1024, 1024], P('fsdp'), may hold values from 10485.76 to 41287.68
- gate_second: float32 [1024, 4608], P('fsdp'), may hold values from 137.6256 to 557.056
- up_second: float32 [1024, 4608], P('fsdp'), may hold values from 137.6256 to 557.056
- down_second: float32 [4608, 1024], P('fsdp'), may hold values from 720.896 to 2883.584
- small_second: float32 [5, 1024], P(None, 'fsdp'), may hold values from 6881.28 to 27525.12
Outputs:
- block_output: bfloat16 [2, 16384, 1024], P(None, ('dp', 'fsdp'))
- input_grad: float32 [2, 16384, 1024], P(None, ('dp', 'fsdp'))
- new_in_weight: float32 [1024, 3072], P('fsdp')
- new_out_weight: float32 [1024, 1024], P('fsdp')
- new_gate_weight: float32 [1024, 4608], P('fsdp')
- new_up_weight: float32 [1024, 4608], P('fsdp')
- new_down_weight: float32 [4608, 1024], P('fsdp')
- new_small_params: float32 [5, 1024], P(None, 'fsdp')
- new_in_first: float32 [1024, 3072], P('fsdp')
- new_out_first: float32 [1024, 1024], P('fsdp')
- new_gate_first: float32 [1024, 4608], P('fsdp')
- new_up_first: float32 [1024, 4608], P('fsdp')
- new_down_first: float32 [4608, 1024], P('fsdp')
- new_small_first: float32 [5, 1024], P(None, 'fsdp')
- new_in_second: float32 [1024, 3072], P('fsdp')
- new_out_second: float32 [1024, 1024], P('fsdp')
- new_gate_second: float32 [1024, 4608], P('fsdp')
- new_up_second: float32 [1024, 4608], P('fsdp')
- new_down_second: float32 [4608, 1024], P('fsdp')
- new_small_second: float32 [5, 1024], P(None, 'fsdp')
All inputs are finite; a program needn't handle non-finite values.
Results may differ from a plain program's by a relative error of at most 0.023.
Values may be sent and summed in bfloat16 or wider, within the bound.
A program may use at most 192 MiB of HBM per device.

v0:
```python
import jax
import jax.numpy as jnp
from jax import lax
from jax.sharding import PartitionSpec as P

KW = 3
MICRO = 2
STEP = 10


norm_eps = 1e-05
beta_one = 0.9
beta_two = 0.95
adam_eps = 1e-08
rate_matrix = 0.02
rate_small = 0.4
weight_decay = 0.1


def from_behind(value, axis, steps):
    count = lax.axis_size(axis)
    leading, last = (max(0, -steps), min(count, count - steps))
    return lax.ppermute(value, axis, [(source, source + steps) for source in range(leading, last)])


def product_nt(left, right):
    return lax.dot_general(
        left, right, (((1,), (1,)), ((), ())), preferred_element_type=jnp.float32
    )


def product_tn(left, right):
    return lax.dot_general(
        left, right, (((0,), (0,)), ((), ())), preferred_element_type=jnp.float32
    )


def norm_back(grad_normed, field, scale, gain):
    normed = field * scale
    weighted = grad_normed * gain
    grad_field = scale * (weighted - normed * jnp.mean(weighted * normed, axis=-1, keepdims=True))
    return (grad_field, jnp.sum(grad_normed * normed, axis=0))


def adam_update(weight, first, second, gradient, step_rate, decay_rate):
    first_new = beta_one * first + (1.0 - beta_one) * gradient
    second_new = beta_two * second + (1.0 - beta_two) * gradient * gradient
    corrected = (
        first_new
        / (1.0 - beta_one**STEP)
        / (jnp.sqrt(second_new / (1.0 - beta_two**STEP)) + adam_eps)
    )
    return (weight - step_rate * (corrected + decay_rate * weight), first_new, second_new)


def body(
    block_input,
    cotangent,
    in_weight,
    out_weight,
    gate_weight,
    up_weight,
    down_weight,
    small_params,
    in_first,
    out_first,
    gate_first,
    up_first,
    down_first,
    small_first,
    in_second,
    out_second,
    gate_second,
    up_second,
    down_second,
    small_second,
):
    position = lax.axis_index("fsdp")
    group_size = lax.axis_size("fsdp")
    keep_tail = (position != 0).astype(jnp.float32)
    keep_head = (position != group_size - 1).astype(jnp.float32)
    row_count = block_input.shape[1]
    model_width = block_input.shape[2]
    totals = None
    outputs = []
    grads_in = []
    for micro_index in range(MICRO):
        gathered = (
            lax.all_gather(in_weight.astype(jnp.bfloat16), "fsdp", axis=0, tiled=True),
            lax.all_gather(out_weight.astype(jnp.bfloat16), "fsdp", axis=0, tiled=True),
            lax.all_gather(gate_weight.astype(jnp.bfloat16), "fsdp", axis=0, tiled=True),
            lax.all_gather(up_weight.astype(jnp.bfloat16), "fsdp", axis=0, tiled=True),
            lax.all_gather(down_weight.astype(jnp.bfloat16), "fsdp", axis=0, tiled=True),
            lax.all_gather(small_params.astype(jnp.bfloat16), "fsdp", axis=1, tiled=True),
        )
        in_low, out_low, gate_low, up_low, down_low, small_low = gathered
        conv_taps = small_low[0:KW].astype(jnp.float32)
        gain_first = small_low[KW].astype(jnp.float32)
        gain_second = small_low[KW + 1].astype(jnp.float32)
        tokens_in = block_input[micro_index].astype(jnp.float32)
        scale_first = lax.rsqrt(jnp.mean(tokens_in * tokens_in, axis=-1, keepdims=True) + norm_eps)
        normed_first = (tokens_in * scale_first * gain_first).astype(jnp.bfloat16)
        projected = jnp.dot(normed_first, in_low, preferred_element_type=jnp.float32)
        gate_b = projected[:, 0:model_width]
        gate_c = projected[:, model_width : 2 * model_width]
        values = projected[:, 2 * model_width : 3 * model_width]
        mixed_in = (gate_b * values).astype(jnp.bfloat16)
        tail_rows = from_behind(mixed_in[row_count - (KW - 1) :], "fsdp", 1)
        extended = jnp.concatenate(
            [tail_rows.astype(jnp.float32) * keep_tail, mixed_in.astype(jnp.float32)], axis=0
        )
        conv_out = jnp.zeros((row_count, model_width), jnp.float32)
        for offset in range(KW):
            conv_out = (
                conv_out
                + conv_taps[offset] * extended[KW - 1 - offset : KW - 1 - offset + row_count]
            )
        gated_out = (gate_c * conv_out).astype(jnp.bfloat16)
        middle = tokens_in + jnp.dot(gated_out, out_low, preferred_element_type=jnp.float32)
        scale_second = lax.rsqrt(jnp.mean(middle * middle, axis=-1, keepdims=True) + norm_eps)
        normed_second = (middle * scale_second * gain_second).astype(jnp.bfloat16)
        gate_pre = jnp.dot(normed_second, gate_low, preferred_element_type=jnp.float32)
        up_pre = jnp.dot(normed_second, up_low, preferred_element_type=jnp.float32)
        gate_sigmoid = jax.nn.sigmoid(gate_pre)
        gate_silu = gate_pre * gate_sigmoid
        hidden_act = (gate_silu * up_pre).astype(jnp.bfloat16)
        block_out = middle + jnp.dot(hidden_act, down_low, preferred_element_type=jnp.float32)
        outputs.append(block_out.astype(jnp.bfloat16))
        in_back, out_back, gate_back, up_back, down_back = (
            lax.all_gather(in_weight.astype(jnp.bfloat16), "fsdp", axis=0, tiled=True),
            lax.all_gather(out_weight.astype(jnp.bfloat16), "fsdp", axis=0, tiled=True),
            lax.all_gather(gate_weight.astype(jnp.bfloat16), "fsdp", axis=0, tiled=True),
            lax.all_gather(up_weight.astype(jnp.bfloat16), "fsdp", axis=0, tiled=True),
            lax.all_gather(down_weight.astype(jnp.bfloat16), "fsdp", axis=0, tiled=True),
        )
        grad_out = cotangent[micro_index]
        grad_hidden = product_nt(grad_out, down_back)
        grad_down = product_tn(hidden_act, grad_out)
        grad_gate = (
            grad_hidden * up_pre * gate_sigmoid * (1.0 + gate_pre * (1.0 - gate_sigmoid))
        ).astype(jnp.bfloat16)
        grad_up = (grad_hidden * gate_silu).astype(jnp.bfloat16)
        grad_second = product_nt(grad_gate, gate_back) + product_nt(grad_up, up_back)
        grad_gate_weight = product_tn(normed_second, grad_gate)
        grad_up_weight = product_tn(normed_second, grad_up)
        grad_middle_norm, grad_gain_second = norm_back(
            grad_second, middle, scale_second, gain_second
        )
        grad_middle = grad_out.astype(jnp.float32) + grad_middle_norm
        grad_branch = grad_middle.astype(jnp.bfloat16)
        grad_out_weight = product_tn(gated_out, grad_branch)
        grad_gated = product_nt(grad_branch, out_back)
        grad_c = grad_gated * conv_out
        grad_conv = (grad_gated * gate_c).astype(jnp.bfloat16)
        head_rows = from_behind(grad_conv[0 : KW - 1], "fsdp", -1)
        conv_wide = grad_conv.astype(jnp.float32)
        grad_extended = jnp.concatenate(
            [conv_wide, head_rows.astype(jnp.float32) * keep_head], axis=0
        )
        grad_mixed = jnp.zeros((row_count, model_width), jnp.float32)
        tap_grads = []
        for offset in range(KW):
            grad_mixed = grad_mixed + conv_taps[offset] * grad_extended[offset : offset + row_count]
            tap_grads.append(
                jnp.sum(conv_wide * extended[KW - 1 - offset : KW - 1 - offset + row_count], axis=0)
            )
        grad_projected = jnp.concatenate(
            [grad_mixed * values, grad_c, grad_mixed * gate_b], axis=1
        ).astype(jnp.bfloat16)
        grad_in_weight = product_tn(normed_first, grad_projected)
        grad_first = product_nt(grad_projected, in_back)
        grad_first_norm, grad_gain_first = norm_back(grad_first, tokens_in, scale_first, gain_first)
        grads_in.append(grad_middle + grad_first_norm)
        grad_small = jnp.stack(tap_grads + [grad_gain_first, grad_gain_second])
        fresh_terms = (
            grad_in_weight,
            grad_out_weight,
            grad_gate_weight,
            grad_up_weight,
            grad_down,
            grad_small,
        )
        if totals is None:
            totals = tuple(fresh_terms)
        else:
            totals = tuple(
                (running + fresh_term for running, fresh_term in zip(totals, fresh_terms))
            )
    totals = (
        lax.psum_scatter(
            totals[0].astype(jnp.bfloat16), "fsdp", scatter_dimension=0, tiled=True
        ).astype(jnp.float32),
        lax.psum_scatter(
            totals[1].astype(jnp.bfloat16), "fsdp", scatter_dimension=0, tiled=True
        ).astype(jnp.float32),
        lax.psum_scatter(
            totals[2].astype(jnp.bfloat16), "fsdp", scatter_dimension=0, tiled=True
        ).astype(jnp.float32),
        lax.psum_scatter(
            totals[3].astype(jnp.bfloat16), "fsdp", scatter_dimension=0, tiled=True
        ).astype(jnp.float32),
        lax.psum_scatter(
            totals[4].astype(jnp.bfloat16), "fsdp", scatter_dimension=0, tiled=True
        ).astype(jnp.float32),
        lax.psum_scatter(
            totals[5].astype(jnp.bfloat16), "fsdp", scatter_dimension=1, tiled=True
        ).astype(jnp.float32),
    )
    summed = lax.psum((totals[0], totals[1], totals[2], totals[3], totals[4], totals[5]), "dp")
    new_in = adam_update(in_weight, in_first, in_second, summed[0], rate_matrix, weight_decay)
    new_out = adam_update(out_weight, out_first, out_second, summed[1], rate_matrix, weight_decay)
    new_gate = adam_update(
        gate_weight, gate_first, gate_second, summed[2], rate_matrix, weight_decay
    )
    new_up = adam_update(up_weight, up_first, up_second, summed[3], rate_matrix, weight_decay)
    new_down = adam_update(
        down_weight, down_first, down_second, summed[4], rate_matrix, weight_decay
    )
    new_small = adam_update(small_params, small_first, small_second, summed[5], rate_small, 0.0)
    return (
        jnp.stack(outputs),
        jnp.stack(grads_in),
        new_in[0],
        new_out[0],
        new_gate[0],
        new_up[0],
        new_down[0],
        new_small[0],
        new_in[1],
        new_out[1],
        new_gate[1],
        new_up[1],
        new_down[1],
        new_small[1],
        new_in[2],
        new_out[2],
        new_gate[2],
        new_up[2],
        new_down[2],
        new_small[2],
    )


def solution(mesh):
    in_specs = (
        P(None, ("dp", "fsdp"), None),
        P(None, ("dp", "fsdp"), None),
        P("fsdp", None),
        P("fsdp", None),
        P("fsdp", None),
        P("fsdp", None),
        P("fsdp", None),
        P(None, "fsdp"),
        P("fsdp", None),
        P("fsdp", None),
        P("fsdp", None),
        P("fsdp", None),
        P("fsdp", None),
        P(None, "fsdp"),
        P("fsdp", None),
        P("fsdp", None),
        P("fsdp", None),
        P("fsdp", None),
        P("fsdp", None),
        P(None, "fsdp"),
    )
    out_specs = (
        P(None, ("dp", "fsdp"), None),
        P(None, ("dp", "fsdp"), None),
        P("fsdp", None),
        P("fsdp", None),
        P("fsdp", None),
        P("fsdp", None),
        P("fsdp", None),
        P(None, "fsdp"),
        P("fsdp", None),
        P("fsdp", None),
        P("fsdp", None),
        P("fsdp", None),
        P("fsdp", None),
        P(None, "fsdp"),
        P("fsdp", None),
        P("fsdp", None),
        P("fsdp", None),
        P("fsdp", None),
        P("fsdp", None),
        P(None, "fsdp"),
    )
    return jax.shard_map(body, mesh=mesh, in_specs=in_specs, out_specs=out_specs, check_vma=False)
```

profile of v0, /device:TPU:0, one launch (start us, length us, event | category | flops | bytes accessed | tf_op | source)
XLA Modules:
  0.0 962.8 jit_solution(1987557278882366688)
XLA Ops:
  7.3 1.8 convert_element_type.194
  9.2 1.5 convert_element_type.201
  10.8 1.8 convert_element_type.203
  14.4 25.6 %all-gather = bf16[32,32,5]{1,2,0:T(8,128)(2,1)S(1)} all-gather(bf16[1,32,5]{1,2,0:T(8,128)(2,1)S(1)} %convert_bitcast_fusion), channel_id=1, replica_groups=mesh['dp'=4,'fsdp'=32] {'fsdp'}, dimensions={0}, use_global_device_ids=true | all-gather | bytes 10560 | tf_op jit(solution)/shard_map/all_gather | solution.py:94
  40.4 22.3 %all-gather.7.cloned.1.call-done = bf16[1024,3072]{1,0:T(8,128)(2,1)} async-done(((bf16[32,3072]{1,0:T(8,128)(2,1)}), bf16[1024,3072]{1,0:T(8,128)(2,1)}) %all-gather.7.cloned.1.call-update) | async-done | bytes 6291472 | tf_op jit(solution)/shard_map/all_gather | solution.py:89
  62.7 4.0 fusion.69
  67.6 2.1 collective-permute-start.1
  71.0 3.0 collective-permute-start
  75.7 32.7 %all-gather.9.cloned.1.call-done = bf16[1024,1024]{1,0:T(8,128)(2,1)} async-done(((bf16[32,1024]{1,0:T(8,128)(2,1)}), bf16[1024,1024]{1,0:T(8,128)(2,1)}) %all-gather.9.cloned.1.call-update) | async-done | bytes 2097168 | tf_op jit(solution)/shard_map/all_gather | solution.py:90
  108.4 3.0 multiply_reduce_fusion.10
  113.1 52.9 %all-gather.11.cloned.1.call-done = bf16[1024,4608]{1,0:T(8,128)(2,1)} async-done(((bf16[32,4608]{1,0:T(8,128)(2,1)}), bf16[1024,4608]{1,0:T(8,128)(2,1)}) %all-gather.11.cloned.1.call-update) | async-done | bytes 9437200 | tf_op jit(solution)/shard_map/all_gather | solution.py:91
  166.0 5.1 fusion.90
  171.1 52.6 %all-gather.13.cloned.1.call-done = bf16[1024,4608]{1,0:T(8,128)(2,1)} async-done(((bf16[32,4608]{1,0:T(8,128)(2,1)}), bf16[1024,4608]{1,0:T(8,128)(2,1)}) %all-gather.13.cloned.1.call-update) | async-done | bytes 9437200 | tf_op jit(solution)/shard_map/all_gather | solution.py:92
  223.7 6.5 fusion.91
  230.3 51.2 %all-gather.15.cloned.1.call-done = bf16[4608,1024]{1,0:T(8,128)(2,1)} async-done(((bf16[144,1024]{1,0:T(8,128)(2,1)}), bf16[4608,1024]{1,0:T(8,128)(2,1)}) %all-gather.15.cloned.1.call-update) | async-done | bytes 9437200 | tf_op jit(solution)/shard_map/all_gather | solution.py:93
  281.5 9.4 multiply_convert_fusion.2
  290.9 7.2 fusion.94
  298.2 6.0 multiply_reduce_fusion.4
  304.1 5.2 fusion.93
  309.4 1.6 fusion.92
  311.1 8.5 multiply_convert_fusion
  319.6 3.1 fusion.95
  322.8 7.1 multiply_reduce_fusion
  334.2 2.7 fusion.64
  339.1 1.6 collective-permute-start.2
  340.8 2.1 collective-permute-done.2
  343.6 2.2 fusion.46
  345.9 3.0 fusion.33
  350.0 4.2 add_convert_fusion.4
  354.3 3.0 fusion.47
  357.4 4.6 add_convert_fusion.3
  363.0 9.3 fusion.97
  372.3 10.9 %add_convert_fusion.1 = bf16[1024,4608]{1,0:T(8,128)(2,1)} fusion(f32[1024,4608]{1,0:T(8,128)} %fusion.97, bf16[128,1024]{1,0:T(8,128)(2,1)S(1)} %copy-done.17, bf16[128,4608]{1,0:T(8,128)(2,1)S(1)} %copy-done.27), kind=kOutput, calls=%fused_computation.1 | convolution fusion | flops 1217396736 | bytes 29753344 | tf_op jit(solution)/shard_map/dot_general | solution.py:33
  383.5 9.2 fusion.96
  392.7 10.7 %add_convert_fusion.2 = bf16[1024,4608]{1,0:T(8,128)(2,1)} fusion(f32[1024,4608]{1,0:T(8,128)} %fusion.96, bf16[128,1024]{1,0:T(8,128)(2,1)S(1)} %copy-done.17, bf16[128,4608]{1,0:T(8,128)(2,1)S(1)} %copy-done.25), kind=kOutput, calls=%fused_computation.2 | convolution fusion | flops 1217396736 | bytes 29753344 | tf_op jit(solution)/shard_map/dot_general | solution.py:33
  404.5 9.2 fusion.52
  413.7 10.7 %add_convert_fusion = bf16[4608,1024]{1,0:T(8,128)(2,1)} fusion(f32[4608,1024]{1,0:T(8,128)} %fusion.52, bf16[128,4608]{1,0:T(8,128)(2,1)S(1)} %copy-done.20, bf16[2,128,1024]{2,1,0:T(8,128)(2,1)S(1)} %copy-done.44), kind=kOutput, calls=%fused_computation | convolution fusion | flops 1217396736 | bytes 29753344 | tf_op jit(solution)/shard_map/dot_general | solution.py:33
  424.4 5.6 fusion.4
  431.5 1.5 fusion.5
  436.1 76.1 %reduce-scatter.11.cloned.1.call-done = bf16[32,1024]{1,0:T(8,128)(2,1)} async-done(((bf16[1024,1024]{1,0:T(8,128)(2,1)}), bf16[32,1024]{1,0:T(8,128)(2,1)}) %reduce-scatter.11.cloned.1.call-update) | async-done | bytes 65552 | tf_op jit(solution)/shard_map/reduce_scatter | solution.py:193
  512.2 89.4 %reduce-scatter.9.cloned.1.call-done = bf16[32,3072]{1,0:T(8,128)(2,1)} async-done(((bf16[1024,3072]{1,0:T(8,128)(2,1)}), bf16[32,3072]{1,0:T(8,128)(2,1)}) %reduce-scatter.9.cloned.1.call-update) | async-done | bytes 196624 | tf_op jit(solution)/shard_map/reduce_scatter | solution.py:190
  601.6 99.0 %reduce-scatter.15.cloned.1.call-done = bf16[32,4608]{1,0:T(8,128)(2,1)} async-done(((bf16[1024,4608]{1,0:T(8,128)(2,1)}), bf16[32,4608]{1,0:T(8,128)(2,1)}) %reduce-scatter.15.cloned.1.call-update) | async-done | bytes 294928 | tf_op jit(solution)/shard_map/reduce_scatter | solution.py:199
  700.7 98.5 %reduce-scatter.13.cloned.1.call-done = bf16[32,4608]{1,0:T(8,128)(2,1)} async-done(((bf16[1024,4608]{1,0:T(8,128)(2,1)}), bf16[32,4608]{1,0:T(8,128)(2,1)}) %reduce-scatter.13.cloned.1.call-update) | async-done | bytes 294928 | tf_op jit(solution)/shard_map/reduce_scatter | solution.py:196
  799.2 99.1 %reduce-scatter.17.cloned.1.call-done = bf16[144,1024]{1,0:T(8,128)(2,1)} async-done(((bf16[4608,1024]{1,0:T(8,128)(2,1)}), bf16[144,1024]{1,0:T(8,128)(2,1)}) %reduce-scatter.17.cloned.1.call-update) | async-done | bytes 294928 | tf_op jit(solution)/shard_map/reduce_scatter | solution.py:202
  898.2 47.7 %all-reduce.2 = (f32[32,3072]{1,0:T(8,128)}, f32[32,1024]{1,0:T(8,128)S(1)}, f32[32,4608]{1,0:T(8,128)}, f32[32,4608]{1,0:T(8,128)}, f32[144,1024]{1,0:T(8,128)}, /*index=5*/f32[5,32]{1,0:T(8,128)S(1)}) all-reduce(bf16[32,3072]{1,0:T(8,128)(2,1)} %reduce-scatter.9.cloned.1.call-done, ...), channel_id=1, replica_groups=mesh['dp'=4,'fsdp'=32] {'dp'}, use_global_device_ids=true, to_apply=%region_9.0 | all-reduce | flops 573600 | bytes 3441600 | tf_op jit(solution)/shard_map/psum | solution.py:209
  945.9 2.6 multiply_subtract_fusion
  948.6 2.7 multiply_subtract_fusion.1
  951.4 1.5 multiply_subtract_fusion.2
  (291 shorter events, 25.4 us)
Async XLA Ops:
  7.2 32.8 %copy-start.4 = (bf16[2,128,1024]{2,1,0:T(8,128)(2,1)S(1)}, bf16[2,128,1024]{2,1,0:T(8,128)(2,1)}, u32[]{:S(2)}) copy-start(bf16[2,128,1024]{2,1,0:T(8,128)(2,1)} %param.20) | copy-start | bytes 1572868
  7.2 55.4 %all-gather.7.cloned.1.call-start = ((), (), s32[]{:S(2)}) async-start(), calls=%async_computation.6 | async-start | bytes 6488064 | tf_op jit(solution)/shard_map/all_gather | solution.py:89
  9.1 99.3 %all-gather.9.cloned.1.call-start = ((), (), s32[]{:S(2)}) async-start(), calls=%async_computation.7 | async-start | bytes 2162688 | tf_op jit(solution)/shard_map/all_gather | solution.py:90
  10.7 155.3 %all-gather.11.cloned.1.call-start = ((), (), s32[]{:S(2)}) async-start(), calls=%async_computation.8 | async-start | bytes 9732096 | tf_op jit(solution)/shard_map/all_gather | solution.py:91
  12.6 211.1 %all-gather.13.cloned.1.call-start = ((), (), s32[]{:S(2)}) async-start(), calls=%async_computation.9 | async-start | bytes 9732096 | tf_op jit(solution)/shard_map/all_gather | solution.py:92
  13.4 268.0 %all-gather.15.cloned.1.call-start = ((), (), s32[]{:S(2)}) async-start(), calls=%async_computation.10 | async-start | bytes 9732096 | tf_op jit(solution)/shard_map/all_gather | solution.py:93
  14.3 421.0 %reduce-scatter.19.cloned.1.call-start = ((), (), s32[]{:S(2)}) async-start(), calls=%async_computation.16 | async-start | bytes 270336
  40.3 26.4 %copy-start.87 = (f32[128]{0:T(128)}, f32[128]{0:T(128)S(1)}, u32[]{:S(2)}) copy-start(f32[128]{0:T(128)S(1)} %add_rsqrt_fusion.1) | copy-start | bytes 1540
  40.3 29.5 %copy-start.85 = (f32[128]{0:T(128)}, f32[128]{0:T(128)S(1)}, u32[]{:S(2)}) copy-start(f32[128]{0:T(128)S(1)} %add_rsqrt_fusion.3) | copy-start | bytes 1540
  40.4 34.0 %copy-start.78 = (f32[1,1024]{1,0:T(1,128)}, f32[1,1024]{1,0:T(1,128)S(1)}, u32[]{:S(2)}) copy-start(f32[1,1024]{1,0:T(1,128)S(1)} %get-tuple-element.91) | copy-start | bytes 12292
  40.4 34.0 %copy-start.80 = (f32[1,1024]{1,0:T(1,128)}, f32[1,1024]{1,0:T(1,128)S(1)}, u32[]{:S(2)}) copy-start(f32[1,1024]{1,0:T(1,128)S(1)} %get-tuple-element.92) | copy-start | bytes 12292
  66.7 7.7 copy-start.6
  66.8 7.6 copy-start.30
  67.6 6.4 collective-permute-start.1
  71.0 3.3 collective-permute-start
  74.0 37.4 %copy-start.76 = (f32[2,1024]{1,0:T(2,128)}, f32[2,1024]{1,0:T(2,128)S(1)}, u32[]{:S(2)}) copy-start(f32[2,1024]{1,0:T(2,128)S(1)} %convert_multiply_fusion.6) | copy-start | bytes 24580
  74.3 37.1 %copy-start.74 = (f32[2,1024]{1,0:T(2,128)}, f32[2,1024]{1,0:T(2,128)S(1)}, u32[]{:S(2)}) copy-start(f32[2,1024]{1,0:T(2,128)S(1)} %convert_multiply_fusion.7) | copy-start | bytes 24580
  75.7 36.2 %copy-start.32 = (bf16[128,1024]{1,0:T(8,128)(2,1)}, bf16[128,1024]{1,0:T(8,128)(2,1)S(1)}, u32[]{:S(2)}) copy-start(bf16[128,1024]{1,0:T(8,128)(2,1)S(1)} %get-tuple-element.95) | copy-start | bytes 786436
  75.7 36.2 %copy-start.39 = (bf16[128,1024]{1,0:T(8,128)(2,1)}, bf16[128,1024]{1,0:T(8,128)(2,1)S(1)}, u32[]{:S(2)}) copy-start(bf16[128,1024]{1,0:T(8,128)(2,1)S(1)} %get-tuple-element.68) | copy-start | bytes 786436
  113.1 110.6 %copy-start.18 = (bf16[128,1024]{1,0:T(8,128)(2,1)}, bf16[128,1024]{1,0:T(8,128)(2,1)S(1)}, u32[]{:S(2)}) copy-start(bf16[128,1024]{1,0:T(8,128)(2,1)S(1)} %multiply_convert_fusion.17) | copy-start | bytes 786436
  171.1 110.3 %copy-start.41 = (bf16[2,128,1024]{2,1,0:T(8,128)(2,1)S(1)}, bf16[2,128,1024]{2,1,0:T(8,128)(2,1)}, u32[]{:S(2)}) copy-start(bf16[2,128,1024]{2,1,0:T(8,128)(2,1)} %param.21) | copy-start | bytes 1572868
  290.8 7.3 copy-start.23
  290.8 7.3 copy-start
  290.8 7.3 copy-start.11
  290.8 7.3 copy-start.13
  290.8 7.3 copy-start.89
  290.9 7.3 copy-start.92
  298.2 11.2 %slice-start = ((s8[9437184]{0:T(1024)(128)(4,1)}), s8[4194304]{0:T(1024)(128)(4,1)S(1)}, s32[]{:S(2)}) async-start(s8[9437184]{0:T(1024)(128)(4,1)} %bitcast.112), calls=%async_computation.17 | async-start | bytes 8388608
  298.2 11.2 %slice-start.1 = ((s8[9437184]{0:T(1024)(128)(4,1)}), s8[4194304]{0:T(1024)(128)(4,1)S(1)}, s32[]{:S(2)}) async-start(s8[9437184]{0:T(1024)(128)(4,1)} %bitcast.112), calls=%async_computation.18 | async-start | bytes 8388608
  330.3 19.7 %copy-start.21 = (f32[128,1024]{1,0:T(8,128)}, f32[128,1024]{1,0:T(8,128)S(1)}, u32[]{:S(2)}) copy-start(f32[128,1024]{1,0:T(8,128)S(1)} %get-tuple-element.85) | copy-start | bytes 1572868
  332.8 10.7 %copy-start.53 = (bf16[128,1024]{1,0:T(8,128)(2,1)}, bf16[128,1024]{1,0:T(8,128)(2,1)S(1)}, u32[]{:S(2)}) copy-start(bf16[128,1024]{1,0:T(8,128)(2,1)S(1)} %get-tuple-element.87) | copy-start | bytes 786436
  332.9 7.9 collective-permute-start.3
  334.2 9.3 slice-start.6
  339.1 3.8 collective-permute-start.2
  349.9 162.3 %reduce-scatter.11.cloned.1.call-start = ((), (), s32[]{:S(2)}) async-start(), calls=%async_computation.12 | async-start | bytes 2162688 | tf_op jit(solution)/shard_map/reduce_scatter | solution.py:193
  354.3 247.3 %reduce-scatter.9.cloned.1.call-start = ((), (), s32[]{:S(2)}) async-start(), calls=%async_computation.11 | async-start | bytes 6488064 | tf_op jit(solution)/shard_map/reduce_scatter | solution.py:190
  362.1 10.2 %copy-start.17 = (bf16[128,1024]{1,0:T(8,128)(2,1)S(1)}, bf16[128,1024]{1,0:T(8,128)(2,1)}, u32[]{:S(2)}) copy-start(bf16[128,1024]{1,0:T(8,128)(2,1)} %copy-done.16) | copy-start | bytes 786436
  362.1 338.6 %reduce-scatter.15.cloned.1.call-start = ((), (), s32[]{:S(2)}) async-start(), calls=%async_computation.14 | async-start | bytes 9732096 | tf_op jit(solution)/shard_map/reduce_scatter | solution.py:199
  363.0 9.3 copy-start.27
  383.2 415.9 %reduce-scatter.13.cloned.1.call-start = ((), (), s32[]{:S(2)}) async-start(), calls=%async_computation.13 | async-start | bytes 9732096 | tf_op jit(solution)/shard_map/reduce_scatter | solution.py:196
  383.5 9.2 copy-start.25
  403.5 494.7 %reduce-scatter.17.cloned.1.call-start = ((), (), s32[]{:S(2)}) async-start(), calls=%async_computation.15 | async-start | bytes 9732096 | tf_op jit(solution)/shard_map/reduce_scatter | solution.py:202
  404.5 9.2 copy-start.20
  434.2 511.7 %copy-start.35 = (f32[144,1024]{1,0:T(8,128)S(1)}, f32[144,1024]{1,0:T(8,128)}, u32[]{:S(2)}) copy-start(f32[144,1024]{1,0:T(8,128)} %param.26) | copy-start | bytes 1769476
  434.2 511.7 %copy-start.58 = (f32[144,1024]{1,0:T(8,128)S(1)}, f32[144,1024]{1,0:T(8,128)}, u32[]{:S(2)}) copy-start(f32[144,1024]{1,0:T(8,128)} %param.32) | copy-start | bytes 1769476
  434.2 511.7 %copy-start.59 = (f32[144,1024]{1,0:T(8,128)S(1)}, f32[144,1024]{1,0:T(8,128)}, u32[]{:S(2)}) copy-start(f32[144,1024]{1,0:T(8,128)} %param.38) | copy-start | bytes 1769476
  436.1 512.5 %copy-start.37 = (f32[32,4608]{1,0:T(8,128)S(1)}, f32[32,4608]{1,0:T(8,128)}, u32[]{:S(2)}) copy-start(f32[32,4608]{1,0:T(8,128)} %param.25) | copy-start | bytes 1769476
  436.1 512.5 %copy-start.60 = (f32[32,4608]{1,0:T(8,128)S(1)}, f32[32,4608]{1,0:T(8,128)}, u32[]{:S(2)}) copy-start(f32[32,4608]{1,0:T(8,128)} %param.31) | copy-start | bytes 1769476
  (72 other events, 238.9 us)
Sparse Core Ops, SparseCore 0:
  10.9 51.7 all-gather.6
  65.5 42.8 all-gather.8
  111.2 54.7 all-gather.10
  168.7 54.9 all-gather.12
  226.4 54.9 all-gather.14
  350.1 80.2 reduce-scatter.18
  434.0 78.2 reduce-scatter.10
  515.9 85.6 reduce-scatter.8
  605.9 94.7 reduce-scatter.14
  704.3 94.8 reduce-scatter.12
  803.4 94.7 reduce-scatter.16
where the time goes:
time: 967 us; the launch traced here: 963 us
  waiting for transfers between devices  676 us (70%)
  matrix products  157 us (16%)
  blocking collectives  73.3 us (8%)
  other arithmetic  22.3 us (2%)
  between operations  15.8 us (2%)
    reduce_scatter x1, waiting for transfers between devices, body(): lax.psum_scatter(totals[4].astype(jnp.bfloat16), 'fsdp', scatter_dimensio...  99.1 us
    reduce_scatter x1, waiting for transfers between devices, body(): lax.psum_scatter(totals[3].astype(jnp.bfloat16), 'fsdp', scatter_dimensio...  99 us
    reduce_scatter x1, waiting for transfers between devices, body(): lax.psum_scatter(totals[2].astype(jnp.bfloat16), 'fsdp', scatter_dimensio...  98.5 us
    reduce_scatter x1, waiting for transfers between devices, body(): lax.psum_scatter(totals[0].astype(jnp.bfloat16), 'fsdp', scatter_dimensio...  89.4 us
    reduce_scatter x1, waiting for transfers between devices, body(): lax.psum_scatter(totals[1].astype(jnp.bfloat16), 'fsdp', scatter_dimensio...  76.1 us
    dot_general x10, matrix products, product_tn(): lax.dot_general(left, right, (((0,), (0,)), ((), ())), preferred_element_...  74.6 us
    all_gather x1, waiting for transfers between devices, body(): lax.all_gather(gate_weight.astype(jnp.bfloat16), 'fsdp', axis=0, tiled=True)  52.9 us
    all_gather x1, waiting for transfers between devices, body(): lax.all_gather(up_weight.astype(jnp.bfloat16), 'fsdp', axis=0, tiled=True)  52.6 us
  transfers between devices with their start and end apart: 15, of which 12 were waited for; matrix products, arithmetic and copies ran while one was open for 12% of the time, Pallas kernels for 0%

commit v1 on v0

v1 whole, which is shorter than its diff:
```python
import functools

import jax
import jax.numpy as jnp
from jax import lax
from jax.experimental import pallas as pl
from jax.experimental.pallas import tpu as pltpu
from jax.sharding import PartitionSpec as P

MESH = pl.DeviceIdType.MESH
KW = 3
MICRO = 2
STEP = 10

norm_eps = 1e-05
beta_one = 0.9
beta_two = 0.95
adam_eps = 1e-08
rate_matrix = 0.02
rate_small = 0.4
weight_decay = 0.1

MATS = ("in", "out", "gate", "up", "down")
THIRDS = {"in": 3, "out": 2, "gate": 3, "up": 3, "down": 3}
FULL = {
    "in": (3, 4, 4, 4, 2, 32, 256),
    "out": (4, 4, 4, 2, 2, 16, 256),
    "gate": (3, 4, 4, 4, 2, 32, 384),
    "up": (3, 4, 4, 4, 2, 32, 384),
    "down": (4, 4, 4, 2, 3, 48, 256),
}
OWN = {
    "in": (3, 4, 32, 256),
    "out": (4, 2, 16, 256),
    "gate": (3, 4, 32, 384),
    "up": (3, 4, 32, 384),
    "down": (4, 3, 48, 256),
}
BLOCK = {"in": (32, 256), "out": (16, 256), "gate": (32, 384), "up": (32, 384), "down": (48, 256)}
BY_THIRD = ("in", "gate", "up")
GATHER_ORDER = {0: ("z", "x"), 1: ("x", "y", "z"), 2: ("z", "x", "y")}
SUM_ORDER = {0: ("x", "z", "y"), 1: ("z", "y", "x"), 2: ("y", "x", "z")}
ALL = slice(None)
VMEM_BYTES = 62 * 1024 * 1024


def coords():
    y = lax.axis_index("dp")
    f = lax.axis_index("fsdp")
    return {"y": y, "z": f // 8, "x": (f // 2) % 4, "c": f % 2}


def device(at):
    return (at["y"], at["z"] * 8 + at["x"] * 2 + at["c"])


def shifted(at, axis, by):
    new = dict(at)
    new[axis] = (at[axis] + by) % (2 if axis == "c" else 4)
    return new


def meet(me):
    sem = pltpu.get_barrier_semaphore()
    peers = [shifted(me, "c", 1)] + [shifted(me, a, s) for a in "xyz" for s in (1, 2, 3)]
    for p in peers:
        pl.semaphore_signal(sem, inc=1, device_id=device(p), device_id_type=MESH)
    pl.semaphore_wait(sem, len(peers))


def half_of(name, half):
    if name in BY_THIRD:
        return (ALL if half is None else pl.ds(16 * half, 16), ALL)
    return (ALL, ALL if half is None else pl.ds(128 * half, 128))


def view(ref, name, t, at, half=None):
    tail = half_of(name, half)
    if name in BY_THIRD:
        return ref.at[(t, at["y"], at["z"], at["x"], at["c"]) + tail]
    return ref.at[(at["y"], at["z"], at["x"], at["c"], t) + tail]


def own_view(ref, name, t, q=ALL):
    if name in BY_THIRD:
        return ref.at[t, q]
    return ref.at[q, t]


class Links:
    def __init__(self, me, send_sem, recv_sem):
        self.me, self.send_sem, self.recv_sem = me, send_sem, recv_sem
        self.sent = []

    def send(self, src, dst, axis, by):
        i = len(self.sent)
        cp = pltpu.make_async_remote_copy(
            src,
            dst,
            self.send_sem.at[i],
            self.recv_sem.at[i],
            device_id=device(shifted(self.me, axis, by)),
            device_id_type=MESH,
        )
        cp.start()
        self.sent.append(cp)
        return cp

    def finish(self):
        for cp in self.sent:
            cp.wait_send()


def gather_kernel(*refs):
    own = dict(zip(MATS, refs[:5]))
    small_own = refs[5]
    full = dict(zip(MATS, refs[6:11]))
    small_full, local_sem, send_sem, recv_sem = refs[11:]
    me = coords()
    links = Links(me, send_sem, recv_sem)
    units = [(name, t) for name in MATS for t in range(THIRDS[name])]

    copies = []
    for k, (name, t) in enumerate(units):
        q = ALL if t == 0 else me["y"]
        src, dst = own_view(own[name], name, t, q), view(full[name], name, t, dict(me, y=q))
        copies.append(pltpu.make_async_copy(src, dst, local_sem.at[k]))
    mine = small_full.at[me["z"], me["x"], me["c"]]
    copies.append(pltpu.make_async_copy(small_own, mine, local_sem.at[len(units)]))
    for cp in copies:
        cp.start()
    meet(me)
    for cp in copies:
        cp.wait()

    def send(u, at, axis, by, half=None):
        piece = view(full[u[0]], u[0], u[1], at, half)
        return links.send(piece, piece, axis, by)

    def send_small(at, axis, steps):
        piece = small_full.at[at["z"], at["x"], at["c"]]
        return [links.send(piece, piece, axis, s) for s in steps]

    at_of = {u: dict(me, y=ALL) if u[1] == 0 else dict(me) for u in units}
    small_at = dict(me)
    tail = []
    for phase, small_axis in enumerate("zxc"):
        active = []
        for u in units:
            order = GATHER_ORDER[u[1]]
            p = phase - (3 - len(order))
            if p >= 0:
                active.append((u, order[p], p == len(order) - 1))
        small = send_small(small_at, small_axis, (1,) if small_axis == "c" else (1, 2, 3))
        first = {}
        for u, axis, last in active:
            at = at_of[u]
            first[u] = (send(u, at, axis, 1), send(u, at, axis, 3))
            if last:
                tail.append(send(u, at, "c", 1))
        second = {}
        for u, axis, last in active:
            from_behind, from_ahead = first[u]
            behind, ahead = shifted(at_of[u], axis, 3), shifted(at_of[u], axis, 1)
            from_behind.wait_recv()
            one = send(u, behind, axis, 1, 0)
            if last:
                tail.append(send(u, behind, "c", 1))
            from_ahead.wait_recv()
            two = send(u, ahead, axis, 3, 1)
            if last:
                tail.append(send(u, ahead, "c", 1))
            second[u] = (one, two)
        for cp in small:
            cp.wait_recv()
        small_at = dict(small_at, **{small_axis: ALL})
        for u, axis, last in active:
            for cp in second[u]:
                cp.wait_recv()
            if last:
                tail.append(send(u, shifted(at_of[u], axis, 2), "c", 1))
            at_of[u] = dict(at_of[u], **{axis: ALL})
    for cp in tail:
        cp.wait_recv()
    links.finish()


def pieces(w, name):
    w = w.astype(jnp.bfloat16)
    if name in BY_THIRD:
        return w.reshape(32, 3, 4, -1).transpose(1, 2, 0, 3)
    if name == "out":
        return w.reshape(2, 16, 4, 256).transpose(2, 0, 1, 3)
    return w.reshape(3, 48, 4, 256).transpose(2, 0, 1, 3)


def joined(g, name):
    if name in BY_THIRD:
        return g.transpose(2, 0, 1, 3).reshape(32, -1)
    return g.transpose(1, 2, 0, 3).reshape(-1, 1024)


def gather(weights, small):
    own = [pieces(w, name) for w, name in zip(weights, MATS)]
    small_low = small.astype(jnp.bfloat16).astype(jnp.float32)
    small_own = jnp.pad(small_low, ((0, 3), (0, 96)))
    in_vmem = pl.BlockSpec(memory_space=pltpu.VMEM)
    anywhere = pl.BlockSpec(memory_space=pl.ANY)
    *full, small_full = pl.pallas_call(
        gather_kernel,
        out_shape=[jax.ShapeDtypeStruct(FULL[name], jnp.bfloat16) for name in MATS]
        + [jax.ShapeDtypeStruct((4, 4, 2, 8, 128), jnp.float32)],
        in_specs=[in_vmem] * 6,
        out_specs=[anywhere] * 5 + [in_vmem],
        scratch_shapes=[
            pltpu.SemaphoreType.DMA((16,)),
            pltpu.SemaphoreType.DMA((256,)),
            pltpu.SemaphoreType.DMA((256,)),
        ],
        compiler_params=pltpu.CompilerParams(collective_id=1, has_side_effects=True),
        name="gather_weights",
    )(*own, small_own)
    small_rows = small_full.reshape(32, 8, 128)[:, 0:5, 0:32]
    return full, small_rows.transpose(1, 0, 2).reshape(5, 1024)


def add_blocks(dst, count, *srcs):
    total = 1
    for n in count:
        total *= n

    def step(i, carry):
        idx = []
        rest = i
        for n in reversed(count):
            idx.insert(0, rest % n)
            rest = rest // n
        ref = dst(tuple(idx))
        value = ref[...].astype(jnp.float32)
        for src in srcs:
            value = value + src(tuple(idx))[...].astype(jnp.float32)
        ref[...] = value.astype(jnp.bfloat16)
        return carry

    lax.fori_loop(0, total, step, 0, unroll=min(4, total))


def sum_units():
    return [(name, t) for name in ("gate", "up", "down", "in", "out") for t in range(THIRDS[name])]


def phase_counts(t):
    order = SUM_ORDER[t]
    return [[a for a in "yzx" if a in order[p + 1 :]] for p in range(3)]


def landing(name, t):
    rows, cols = BLOCK[name]
    half = (rows // 2, cols) if name in BY_THIRD else (rows, cols // 2)
    shapes = []
    for rest in phase_counts(t):
        lead = (4,) * len(rest)
        shapes.append(((2,) + lead + half, (2,) + lead + (rows, cols)))
    return shapes


def reduce_kernel(*refs):
    names = MATS
    grads = dict(zip(names, refs[:5]))
    small = refs[5]
    outs = dict(zip(names, refs[6:11]))
    small_out = refs[11]
    scratch = list(refs[12:])
    mine = {name: scratch.pop(0) for name in names}
    theirs = {name: scratch.pop(0) for name in names}
    units = sum_units()
    land = {u: [(scratch.pop(0), scratch.pop(0)) for _ in range(3)] for u in units}
    small_land = scratch.pop(0)
    local_sem, send_sem, recv_sem = scratch
    me = coords()
    links = Links(me, send_sem, recv_sem)
    batches = [[u for u in units if u[0] == name] for name in ("gate", "up", "down", "in", "out")]

    def part(ref, u, at, half=None):
        name, t = u
        tail = half_of(name, half)
        if name in BY_THIRD:
            return ref.at[(t, at["y"], at["z"], at["x"]) + tail]
        return ref.at[(at["y"], at["z"], at["x"], t) + tail]

    every = {"y": ALL, "z": ALL, "x": ALL}
    loads, swaps = {}, {}
    for k, name in enumerate(names):
        pick = (ALL,) * (4 if name in BY_THIRD else 3) + (me["c"],)
        loads[name] = pltpu.make_async_copy(grads[name].at[pick], mine[name], local_sem.at[k])
    meet(me)
    for name in ("gate", "up", "down", "in", "out"):
        loads[name].start()
        pick = (ALL,) * (4 if name in BY_THIRD else 3) + (1 - me["c"],)
        swaps[name] = links.send(grads[name].at[pick], theirs[name], "c", 1)

    small_out[...] = small[...]
    small_pending = []
    small_ids = set()

    def small_send(axis, slot):
        steps = (1,) if axis == "c" else (1, 2, 3)
        small_ids.update(range(len(links.sent), len(links.sent) + len(steps)))
        small_pending.append(
            [links.send(small_out, small_land.at[slot + s - 1], axis, s) for s in steps]
        )

    def small_take(slot):
        pending = small_pending.pop(0)
        for cp in pending:
            cp.wait()
        total = small_out[...]
        for s in range(len(pending)):
            total = total + small_land[slot + s]
        small_out[...] = total

    small_steps = [("c", 0), ("x", 1), ("z", 4), ("y", 7)]

    at_of = {u: dict(every) for u in units}
    pending = {}

    def lead_of(u, p):
        return phase_counts(u[1])[p]

    def adder(u, p, at, half, *landed):
        rest = lead_of(u, p)

        def dst(idx):
            spot = dict(at)
            spot.update(zip(rest, idx))
            return part(mine[u[0]], u, spot, half)

        def src(ref):
            return lambda idx: ref.at[idx] if idx else ref

        add_blocks(dst, (4,) * len(rest), *[src(r) for r in landed])

    def start_phase(u, p):
        axis = SUM_ORDER[u[1]][p]
        far = dict(at_of[u], **{axis: (me[axis] + 2) % 4})
        halves = land[u][p][0]
        pending[u] = [
            links.send(part(mine[u[0]], u, far, 0), halves.at[0], axis, 1),
            links.send(part(mine[u[0]], u, far, 1), halves.at[1], axis, 3),
        ]

    def middle_phase(u, p):
        axis = SUM_ORDER[u[1]][p]
        halves, blocks = land[u][p]
        ahead = dict(at_of[u], **{axis: (me[axis] + 1) % 4})
        behind = dict(at_of[u], **{axis: (me[axis] + 3) % 4})
        one, two = pending[u]
        one.wait_recv()
        adder(u, p, ahead, 0, halves.at[0])
        a = links.send(part(mine[u[0]], u, ahead), blocks.at[0], axis, 1)
        two.wait_recv()
        adder(u, p, behind, 1, halves.at[1])
        b = links.send(part(mine[u[0]], u, behind), blocks.at[1], axis, 3)
        pending[u] = [a, b]

    def end_phase(u, p):
        axis = SUM_ORDER[u[1]][p]
        blocks = land[u][p][1]
        for cp in pending[u]:
            cp.wait_recv()
        at_of[u] = dict(at_of[u], **{axis: me[axis]})
        adder(u, p, at_of[u], None, blocks.at[0], blocks.at[1])

    last = []

    def stage(s, batch):
        name = batch[0][0]
        if s == 0:
            loads[name].wait()
            swaps[name].wait_recv()
            for u in batch:
                t = u[1]

                def dst(idx, u=u):
                    return part(mine[u[0]], u, dict(zip("yzx", idx)))

                def src(idx, u=u):
                    return part(theirs[u[0]], u, dict(zip("yzx", idx)))

                add_blocks(dst, (4, 4, 4), src)
                start_phase(u, 0)
            return
        p, kind = (s - 1) // 2, (s - 1) % 2
        if p < 3:
            for u in batch:
                if kind == 0:
                    middle_phase(u, p)
                else:
                    end_phase(u, p)
                    if p < 2:
                        start_phase(u, p + 1)
                    else:
                        spot = own_view(outs[u[0]], u[0], u[1], me["y"])
                        spot[...] = part(mine[u[0]], u, at_of[u])[...]
                        for by in (1, 2, 3):
                            last.append(links.send(spot, spot, "y", by))

    stages = 7
    small_send(*small_steps[0])
    for tick in range(len(batches) + stages - 1):
        if 0 < tick <= 4:
            small_take(small_steps[tick - 1][1])
            if tick < 4:
                small_send(*small_steps[tick])
        for s in range(stages):
            if 0 <= tick - s < len(batches):
                stage(s, batches[tick - s])
    for cp in last:
        cp.wait_recv()
    for i, cp in enumerate(links.sent):
        if i not in small_ids:
            cp.wait_send()


def sums(grads, small):
    in_vmem = pl.BlockSpec(memory_space=pltpu.VMEM)
    anywhere = pl.BlockSpec(memory_space=pl.ANY)
    core = {}
    for name in MATS:
        shape = list(FULL[name])
        del shape[4 if name in BY_THIRD else 3]
        core[name] = tuple(shape)
    scratch = [pltpu.VMEM(core[name], jnp.bfloat16) for name in MATS] * 2
    for u in sum_units():
        for halves, blocks in landing(*u):
            scratch += [pltpu.VMEM(halves, jnp.bfloat16), pltpu.VMEM(blocks, jnp.bfloat16)]
    scratch += [
        pltpu.VMEM((10, 8, 1024), jnp.float32),
        pltpu.SemaphoreType.DMA((8,)),
        pltpu.SemaphoreType.DMA((256,)),
        pltpu.SemaphoreType.DMA((256,)),
    ]
    *outs, small_sum = pl.pallas_call(
        reduce_kernel,
        out_shape=[jax.ShapeDtypeStruct(OWN[name], jnp.bfloat16) for name in MATS]
        + [jax.ShapeDtypeStruct((8, 1024), jnp.float32)],
        in_specs=[anywhere] * 5 + [in_vmem],
        out_specs=[in_vmem] * 6,
        scratch_shapes=scratch,
        compiler_params=pltpu.CompilerParams(
            collective_id=2, has_side_effects=True, vmem_limit_bytes=VMEM_BYTES
        ),
        name="sum_gradients",
    )(*[g.reshape(FULL[name]) for g, name in zip(grads, MATS)], small)
    return outs, small_sum


def dot_nt(left, right):
    return lax.dot_general(
        left, right, (((1,), (1,)), ((), ())), preferred_element_type=jnp.float32
    )


def dot_nn(left, right):
    return jnp.dot(left, right, preferred_element_type=jnp.float32)


def dot_tn(left, right):
    return lax.dot_general(
        left, right, (((0,), (0,)), ((), ())), preferred_element_type=jnp.float32
    )


def feed_forward_kernel(ns_ref, nst_ref, g_ref, wg_ref, wu_ref, wd_ref, dg_ref, du_ref, dd_ref, out_ref, gs_ref):
    @pl.when(pl.program_id(0) == 0)
    def _():
        out_ref[...] = jnp.zeros_like(out_ref)
        gs_ref[...] = jnp.zeros_like(gs_ref)

    ns = ns_ref[...]
    wg = wg_ref[0]
    wu = wu_ref[0]
    gate_pre = dot_nn(ns, wg)
    up_pre = dot_nn(ns, wu)
    grad_hidden = dot_nt(g_ref[:, 0:256], wd_ref[0])
    for q in range(1, 4):
        grad_hidden += dot_nt(g_ref[:, 256 * q : 256 * q + 256], wd_ref[q])
    sig = jax.nn.sigmoid(gate_pre)
    silu = gate_pre * sig
    hidden = (silu * up_pre).astype(jnp.bfloat16)
    grad_gate = (grad_hidden * up_pre * sig * (1.0 + gate_pre * (1.0 - sig))).astype(jnp.bfloat16)
    grad_up = (grad_hidden * silu).astype(jnp.bfloat16)
    gs_ref[...] += dot_nt(grad_gate, wg) + dot_nt(grad_up, wu)
    nst = nst_ref[...]
    dg_ref[0] = dot_nn(nst, grad_gate).astype(jnp.bfloat16)
    du_ref[0] = dot_nn(nst, grad_up).astype(jnp.bfloat16)
    for q in range(4):
        cols = slice(256 * q, 256 * q + 256)
        out_ref[:, cols] += dot_nn(hidden, wd_ref[q])
        dd_ref[q] = dot_tn(hidden, g_ref[:, cols]).astype(jnp.bfloat16)


def feed_forward(ns, g, wg, wu, wd):
    whole = lambda shape: pl.BlockSpec(shape, lambda j: (0,) * len(shape))
    col = pl.BlockSpec((1, 1024, 384), lambda j: (j, 0, 0))
    row = pl.BlockSpec((4, 384, 256), lambda j: (0, j, 0))
    wide = jax.ShapeDtypeStruct((12, 1024, 384), jnp.bfloat16)
    return pl.pallas_call(
        feed_forward_kernel,
        grid=(12,),
        in_specs=[whole((256, 1024)), whole((1024, 256)), whole((256, 1024)), col, col, row],
        out_specs=[col, col, row, whole((256, 1024)), whole((256, 1024))],
        out_shape=[
            wide,
            wide,
            jax.ShapeDtypeStruct((4, 4608, 256), jnp.bfloat16),
            jax.ShapeDtypeStruct((256, 1024), jnp.float32),
            jax.ShapeDtypeStruct((256, 1024), jnp.float32),
        ],
        compiler_params=pltpu.CompilerParams(vmem_limit_bytes=VMEM_BYTES),
        name="feed_forward",
    )(ns, ns.T, g, wg, wu, wd)


def norm_back(grad_normed, field, scale, gain):
    normed = field * scale
    weighted = grad_normed * gain
    grad_field = scale * (weighted - normed * jnp.mean(weighted * normed, axis=-1, keepdims=True))
    return (grad_field, jnp.sum(grad_normed * normed, axis=0))


def adam_update(weight, first, second, gradient, step_rate, decay_rate):
    first_new = beta_one * first + (1.0 - beta_one) * gradient
    second_new = beta_two * second + (1.0 - beta_two) * gradient * gradient
    corrected = (
        first_new
        / (1.0 - beta_one**STEP)
        / (jnp.sqrt(second_new / (1.0 - beta_two**STEP)) + adam_eps)
    )
    return (weight - step_rate * (corrected + decay_rate * weight), first_new, second_new)


def from_behind(value, axis, steps):
    count = lax.axis_size(axis)
    leading, last = (max(0, -steps), min(count, count - steps))
    return lax.ppermute(value, axis, [(source, source + steps) for source in range(leading, last)])


def body(
    block_input,
    cotangent,
    in_weight,
    out_weight,
    gate_weight,
    up_weight,
    down_weight,
    small_params,
    in_first,
    out_first,
    gate_first,
    up_first,
    down_first,
    small_first,
    in_second,
    out_second,
    gate_second,
    up_second,
    down_second,
    small_second,
):
    position = lax.axis_index("fsdp")
    keep_tail = (position != 0).astype(jnp.float32)
    keep_head = (position != 31).astype(jnp.float32)
    full, small_low = gather(
        (in_weight, out_weight, gate_weight, up_weight, down_weight), small_params
    )
    w_in = full[0].reshape(12, 1024, 256)
    w_out = full[1].reshape(4, 1024, 256)
    w_gate = full[2].reshape(12, 1024, 384)
    w_up = full[3].reshape(12, 1024, 384)
    w_down = full[4].reshape(4, 4608, 256)
    conv_taps = small_low[0:KW]
    gain_first = small_low[KW]
    gain_second = small_low[KW + 1]

    rows = block_input.shape[1]
    tokens = block_input.astype(jnp.float32).reshape(256, 1024)
    scale_first = lax.rsqrt(jnp.mean(tokens * tokens, axis=-1, keepdims=True) + norm_eps)
    normed_first = (tokens * scale_first * gain_first).astype(jnp.bfloat16)
    projected = jnp.einsum("tk,pkn->tpn", normed_first, w_in, preferred_element_type=jnp.float32)
    projected = projected.reshape(256, 3072)
    gate_b = projected[:, 0:1024]
    gate_c = projected[:, 1024:2048]
    values = projected[:, 2048:3072]
    mixed_in = (gate_b * values).astype(jnp.bfloat16).reshape(MICRO, rows, 1024)
    tail_rows = from_behind(mixed_in[:, rows - (KW - 1) :], "fsdp", 1)
    extended = jnp.concatenate(
        [tail_rows.astype(jnp.float32) * keep_tail, mixed_in.astype(jnp.float32)], axis=1
    )
    conv_out = jnp.zeros((MICRO, rows, 1024), jnp.float32)
    for offset in range(KW):
        start = KW - 1 - offset
        conv_out = conv_out + conv_taps[offset] * extended[:, start : start + rows]
    conv_out = conv_out.reshape(256, 1024)
    gated_out = (gate_c * conv_out).astype(jnp.bfloat16)
    branch = jnp.einsum("tk,qkn->tqn", gated_out, w_out, preferred_element_type=jnp.float32)
    middle = tokens + branch.reshape(256, 1024)
    scale_second = lax.rsqrt(jnp.mean(middle * middle, axis=-1, keepdims=True) + norm_eps)
    normed_second = (middle * scale_second * gain_second).astype(jnp.bfloat16)

    grad_out = cotangent.reshape(256, 1024)
    grad_gate_weight, grad_up_weight, grad_down, ff_out, grad_second = feed_forward(
        normed_second, grad_out, w_gate, w_up, w_down
    )
    block_out = (middle + ff_out).astype(jnp.bfloat16)
    grad_middle_norm, grad_gain_second = norm_back(grad_second, middle, scale_second, gain_second)
    grad_middle = grad_out.astype(jnp.float32) + grad_middle_norm
    grad_branch = grad_middle.astype(jnp.bfloat16)
    grad_branch_cut = grad_branch.reshape(256, 4, 1024 // 4)
    grad_out_weight = jnp.einsum(
        "tk,tqn->qkn", gated_out, grad_branch_cut, preferred_element_type=jnp.float32
    )
    grad_gated = jnp.einsum(
        "tqn,qkn->tk", grad_branch_cut, w_out, preferred_element_type=jnp.float32
    )
    grad_c = grad_gated * conv_out
    grad_conv = (grad_gated * gate_c).astype(jnp.bfloat16).reshape(MICRO, rows, 1024)
    head_rows = from_behind(grad_conv[:, 0 : KW - 1], "fsdp", -1)
    conv_wide = grad_conv.astype(jnp.float32)
    grad_extended = jnp.concatenate([conv_wide, head_rows.astype(jnp.float32) * keep_head], axis=1)
    grad_mixed = jnp.zeros((MICRO, rows, 1024), jnp.float32)
    tap_grads = []
    for offset in range(KW):
        start = KW - 1 - offset
        grad_mixed = grad_mixed + conv_taps[offset] * grad_extended[:, offset : offset + rows]
        tap_grads.append(jnp.sum(conv_wide * extended[:, start : start + rows], axis=(0, 1)))
    grad_mixed = grad_mixed.reshape(256, 1024)
    grad_projected = jnp.concatenate(
        [grad_mixed * values, grad_c, grad_mixed * gate_b], axis=1
    ).astype(jnp.bfloat16)
    grad_projected_cut = grad_projected.reshape(256, 12, 256)
    grad_in_weight = jnp.einsum(
        "tk,tpn->pkn", normed_first, grad_projected_cut, preferred_element_type=jnp.float32
    )
    grad_first = jnp.einsum(
        "tpn,pkn->tk", grad_projected_cut, w_in, preferred_element_type=jnp.float32
    )
    grad_first_norm, grad_gain_first = norm_back(grad_first, tokens, scale_first, gain_first)
    input_grad = grad_middle + grad_first_norm
    zero_row = jnp.zeros_like(grad_gain_first)
    grad_small = jnp.stack(tap_grads + [grad_gain_first, grad_gain_second] + [zero_row] * 3)

    summed, small_sum = sums(
        (
            grad_in_weight.astype(jnp.bfloat16),
            grad_out_weight.astype(jnp.bfloat16),
            grad_gate_weight,
            grad_up_weight,
            grad_down,
        ),
        grad_small,
    )
    summed = [joined(g, name).astype(jnp.float32) for g, name in zip(summed, MATS)]
    small_mine = lax.dynamic_slice(small_sum, (0, position * 32), (5, 32))
    new_in = adam_update(in_weight, in_first, in_second, summed[0], rate_matrix, weight_decay)
    new_out = adam_update(out_weight, out_first, out_second, summed[1], rate_matrix, weight_decay)
    new_gate = adam_update(
        gate_weight, gate_first, gate_second, summed[2], rate_matrix, weight_decay
    )
    new_up = adam_update(up_weight, up_first, up_second, summed[3], rate_matrix, weight_decay)
    new_down = adam_update(
        down_weight, down_first, down_second, summed[4], rate_matrix, weight_decay
    )
    new_small = adam_update(small_params, small_first, small_second, small_mine, rate_small, 0.0)
    news = (new_in, new_out, new_gate, new_up, new_down, new_small)
    return (
        block_out.reshape(MICRO, rows, 1024),
        input_grad.reshape(MICRO, rows, 1024),
        *[n[0] for n in news],
        *[n[1] for n in news],
        *[n[2] for n in news],
    )


def solution(mesh):
    acts = P(None, ("dp", "fsdp"), None)
    params = (P("fsdp", None),) * 5 + (P(None, "fsdp"),)
    return jax.shard_map(
        body,
        mesh=mesh,
        in_specs=(acts, acts) + params * 3,
        out_specs=(acts, acts) + params * 3,
        check_vma=False,
    )
```

time: 967 us -> 331 us (0.34)
  waiting for transfers between devices: 676 us -> 0.01 us
  Pallas kernels: 0 us -> 232 us
  matrix products: 157 us -> 20.4 us
  blocking collectives: 73.3 us -> 0 us
  local copies, waits for them, and re-layouts: 9.38 us -> 43.2 us
  between operations: 15.8 us -> 1.47 us
    reduce_scatter x5 -> x0, waiting for transfers between devices: 462 us -> none  [the longest x1 99.1 us: body(): lax.psum_scatter(totals[4].astype(jnp.bfloat16), 'fsdp', scatter_dimensio...]
    pallas_call x0 -> x3, Pallas kernels: none -> 232 us  [the longest x1 107 us: sums(): pl.pallas_call(reduce_kernel, out_shape=[jax.ShapeDtypeStruct(OWN[name],...]
    all_gather x5 -> x0, waiting for transfers between devices: 212 us -> none  [the longest x1 52.9 us: body(): lax.all_gather(gate_weight.astype(jnp.bfloat16), 'fsdp', axis=0, tiled=True)]
    dot_general x30 -> x6, matrix products: 157 us -> 20.4 us  [the longest x1 5.6 us: body(): jnp.einsum('tpn,pkn->tk', grad_projected_cut, w_in, preferred_element_typ...]
    psum x1 -> x0, blocking collectives: 47.7 us -> none  [body(): lax.psum((totals[0], totals[1], totals[2], totals[3], totals[4], totals[5...]
    all_gather x1 -> x0, blocking collectives: 25.6 us -> none  [body(): lax.all_gather(small_params.astype(jnp.bfloat16), 'fsdp', axis=1, tiled=T...]
    convert_element_type x0 -> x10, local copies, waits for them, and re-layouts: none -> 18.4 us  [the longest x1 8.62 us: body(): grad_in_weight.astype(jnp.bfloat16)]
    reshape x0 -> x11, local copies, waits for them, and re-layouts: none -> 16.6 us  [the longest x1 8.74 us: body(): w_in = full[0].reshape(12, 1024, 256)]
  transfers between devices with their start and end apart: 15 -> 2, of which waited for: 12 -> 0; matrix products, arithmetic and copies ran while one was open for 12% -> 3% of each run, Pallas kernels for 0% -> 0%
where the time goes in v1:
time: 331 us; the launch traced here: 328 us
  Pallas kernels  232 us (70%)
  local copies, waits for them, and re-layouts  43.2 us (13%)
  other arithmetic  25.8 us (8%)
  matrix products  20.4 us (6%)
  starting transfers between devices  4.43 us (1%)
    pallas_call x1, Pallas kernels, sums(): pl.pallas_call(reduce_kernel, out_shape=[jax.ShapeDtypeStruct(OWN[name],...  107 us
    pallas_call x1, Pallas kernels, gather(): pl.pallas_call(gather_kernel, out_shape=[jax.ShapeDtypeStruct(FULL[name],...  89.6 us
    pallas_call x1, Pallas kernels, feed_forward(): pl.pallas_call(feed_forward_kernel, grid=(12,), in_specs=[whole((256, 102...  36.2 us
    reshape x1, local copies, waits for them, and re-layouts, body(): w_in = full[0].reshape(12, 1024, 256)  8.74 us
    convert_element_type x1, local copies, waits for them, and re-layouts, body(): grad_in_weight.astype(jnp.bfloat16)  8.62 us
    sub x6, other arithmetic, adam_update(): weight - step_rate * (corrected + decay_rate * weight)  7.9 us
  transfers between devices with their start and end apart: 2, of which 0 were waited for; matrix products, arithmetic and copies ran while one was open for 3% of the time, Pallas kernels for 0%

profile of v1, /device:TPU:0, one launch (start us, length us, event | category | flops | bytes accessed | tf_op | source)
XLA Modules:
  0.0 327.6 jit_solution(8790072998881176924)
XLA Ops:
  0.7 1.3 multiply_reduce_fusion.8
  2.0 1.0 convert_element_type.137
  3.2 0.7 copy.86
  3.9 0.9 convert_element_type.138
  4.8 0.6 copy.87
  6.0 0.7 copy.85
  6.8 0.6 pad_convert_fusion.refs_5_
  7.4 0.9 copy_bitcast_fusion.1
  8.3 89.6 %gather_weights.1 = (bf16[3,4,4,4,2,32,256]{6,5,4,3,2,1,0:T(8,128)(2,1)}, bf16[4,4,4,2,2,16,256]{6,5,4,3,2,1,0:T(8,128)(2,1)}, bf16[3,4,4,4,2,32,384]{6,5,4,3,2,...) custom-call(bf16[3,4,32,256]{3,2,1,0:T(8,128)(2,1)} %bitcast.158, ...), custom_call_target="tpu_custom_call" | custom-call | tf_op jit(solution)/shard_map/gather_weights/pallas_call | solution.py:209
  97.9 0.9 slice_bitcast_fusion
  99.1 8.7 %copy.54 = bf16[12,1024,256]{1,2,0:T(8,128)(2,1)} copy(bf16[12,1024,256]{2,1,0:T(8,128)(2,1)} %bitcast.140) | data formatting | bytes 12582912 | tf_op jit(solution)/shard_map/reshape | solution.py:577
  108.0 4.6 %fusion.26 = f32[256,3072]{1,0:T(8,128)S(1)} fusion(bf16[256,1024]{1,0:T(8,128)(2,1)S(1)} %bitcast.160, bf16[3072,1024]{1,0:T(8,128)(2,1)} %bitcast.142), kind=kOutput, calls=%fused_computation.99 | convolution fusion | flops 1610612736 | bytes 9961472 | tf_op jit(solution)/shard_map/tk,pkn->tpn/dot_general | solution.py:590
  112.7 1.6 copy-done.4
  114.5 2.8 collective-permute-start
  117.5 4.0 %copy.55 = bf16[4,1024,256]{1,2,0:T(8,128)(2,1)} copy(bf16[4,1024,256]{2,1,0:T(8,128)(2,1)} %bitcast.150) | data formatting | bytes 4194304 | tf_op jit(solution)/shard_map/reshape | solution.py:578
  122.0 2.0 fusion.8
  124.0 0.8 multiply_reduce_fusion.7
  124.9 1.0 multiply_convert_fusion.2.ns_ref
  126.0 1.0 copy.56.nst_ref
  127.0 36.2 %feed_forward.1 = (bf16[12,1024,384]{2,1,0:T(8,128)(2,1)}, bf16[12,1024,384]{2,1,0:T(8,128)(2,1)}, bf16[4,4608,256]{2,1,0:T(8,128)(2,1)}, f32[256,1024]{1,0:T(8,128)}, f32[256,1024]{1,0:T(8,128)}) custom-call(bf16[256,1024]{1,0:T(8,128)(2,1)} %multiply_convert_fusion.2.ns_ref, bf16[1024,256]{1,0:T(8,128)(2,1)} %copy.56.nst_ref, bf16[256,1024]{1,0:T(8,128)(2,1)} %bitcast.143, ...), custom_call_target="tpu_custom_call" | custom-call | tf_op jit(solution)/shard_map/feed_forward/pallas_call | solution.py:508
  163.2 1.7 multiply_reduce_fusion
  164.9 1.1 fusion.19
  166.1 1.2 copy.71
  167.3 2.8 multiply_reduce_fusion.2
  170.2 2.1 convert_bitcast_fusion.1
  172.3 1.6 collective-permute-start.1
  174.5 4.0 %copy.64 = bf16[4,1024,256]{2,1,0:T(8,128)(2,1)} copy(bf16[4,1024,256]{1,2,0:T(8,128)(2,1)} %convert_bitcast_fusion.1) | data formatting | bytes 4194304 | tf_op jit(solution)/shard_map/convert_element_type | solution.py:656
  178.8 1.9 fusion.7
  180.9 5.6 %multiply_reduce_fusion.1 = (f32[1024]{0:T(1024)S(1)}, f32[256]{0:T(256)S(1)}, bf16[256,1024]{1,0:T(8,128)(2,1)S(1)}, f32[256,1024]{1,0:T(8,128)}) fusion(bf16[2,128,1024]{2,1,0:T(8,128)(2,1)S(1)} %copy-done.5, f32[256]{0:T(256)S(1)} %get-tuple-element.91, f32[1024]{0:T(1024)S(1)} %mul.387, bf16[256,12,256]{2,0,1:T(8,128)(2,1)S(1)} %bitcast_dynamic-update-slice_fusion, ...), kind=kOutput, calls=%fused_computation.27 | convolution fusion | flops 1612970752 | bytes 9971712 | tf_op jit(solution)/shard_map/tpn,pkn->tk/dot_general | solution.py:645
  186.5 0.6 broadcast_multiply_fusion
  187.0 4.4 %convert_bitcast_fusion = bf16[12,1024,256]{1,2,0:T(8,128)(2,1)} fusion(bf16[256,12,256]{2,0,1:T(8,128)(2,1)S(1)} %bitcast_dynamic-update-slice_fusion, bf16[256,1024]{1,0:T(8,128)(2,1)S(1)} %get-tuple-element.90), kind=kOutput, calls=%fused_computation | convolution fusion | flops 1613758464 | bytes 8388608 | tf_op jit(solution)/shard_map/tk,tpn->pkn/dot_general | solution.py:642
  191.5 8.6 %copy.62 = bf16[12,1024,256]{2,1,0:T(8,128)(2,1)} copy(bf16[12,1024,256]{1,2,0:T(8,128)(2,1)} %convert_bitcast_fusion) | data formatting | bytes 12582912 | tf_op jit(solution)/shard_map/convert_element_type | solution.py:655
  200.1 0.7 stack.27.refs_5_
  200.8 106.5 %sum_gradients.1 = (bf16[3,4,32,256]{3,2,1,0:T(8,128)(2,1)}, bf16[4,2,16,256]{3,2,1,0:T(8,128)(2,1)}, bf16[3,4,32,384]{3,2,1,0:T(8,128)(2,1)}, bf16[3,4,32,384]{...) custom-call(bf16[3,4,4,4,2,32,256]{6,5,4,3,2,1,0:T(8,128)(2,1)} %bitcast.130, ...), custom_call_target="tpu_custom_call" | custom-call | tf_op jit(solution)/shard_map/sum_gradients/pallas_call | solution.py:443
  307.3 1.0 convert_bitcast_fusion.5
  308.9 0.7 copy.75
  310.1 1.1 reshape.227
  311.2 1.2 copy.68
  312.4 2.2 reshape.228
  314.6 1.2 convert_bitcast_fusion.2
  316.4 1.8 multiply_add_fusion
  318.3 1.2 multiply_subtract_fusion.3
  319.5 0.8 multiply_subtract_fusion.4
  320.4 1.5 multiply_subtract_fusion.2
  322.0 0.5 copy-done.28
  322.7 1.5 multiply_subtract_fusion.1
  324.7 1.5 multiply_subtract_fusion
  326.3 1.4 multiply_subtract_fusion.5
  (142 shorter events, 5.7 us)
Async XLA Ops:
  0.7 4.8 %copy-start.15 = (f32[32,4608]{1,0:T(8,128)S(1)}, f32[32,4608]{1,0:T(8,128)}, u32[]{:S(2)}) copy-start(f32[32,4608]{1,0:T(8,128)} %param.25) | copy-start | bytes 1769476
  0.7 4.9 %copy-start.13 = (f32[32,4608]{1,0:T(8,128)S(1)}, f32[32,4608]{1,0:T(8,128)}, u32[]{:S(2)}) copy-start(f32[32,4608]{1,0:T(8,128)} %param.24) | copy-start | bytes 1769476
  2.0 178.9 %copy-start.44 = (f32[256]{0:T(256)}, f32[256]{0:T(256)S(1)}, u32[]{:S(2)}) copy-start(f32[256]{0:T(256)S(1)} %get-tuple-element.91) | copy-start | bytes 3076
  3.0 2.7 copy-start.17
  99.1 8.7 %copy-start.5 = (bf16[2,128,1024]{2,1,0:T(8,128)(2,1)S(1)}, bf16[2,128,1024]{2,1,0:T(8,128)(2,1)}, u32[]{:S(2)}) copy-start(bf16[2,128,1024]{2,1,0:T(8,128)(2,1)} %param.20) | copy-start | bytes 1572868
  112.7 1.6 copy-start.4
  114.5 7.1 %copy-start.21 = (bf16[256,1024]{1,0:T(8,128)(2,1)}, bf16[256,1024]{1,0:T(8,128)(2,1)S(1)}, u32[]{:S(2)}) copy-start(bf16[256,1024]{1,0:T(8,128)(2,1)S(1)} %get-tuple-element.85) | copy-start | bytes 1572868
  114.5 7.1 %copy-start.11 = (f32[2,128,1024]{2,1,0:T(8,128)}, f32[2,128,1024]{2,1,0:T(8,128)S(1)}, u32[]{:S(2)}) copy-start(f32[2,128,1024]{2,1,0:T(8,128)S(1)} %get-tuple-element.84) | copy-start | bytes 3145732
  114.5 7.1 %collective-permute-start = (bf16[2,2,1024]{2,1,0:T(2,128)(2,1)S(1)}, bf16[2,2,1024]{2,1,0:T(2,128)(2,1)S(1)}, u32[]{:S(2)}, u32[]{:S(2)}) collective-permute-start(bf16[2,2,1024]{2,1,0:T(2,128)(2,1)S(1)} %slice.82), channel_id=1, source_target_pairs={{0,1},{1,2},{2,3},{3,4},{4,5},{5,6},{6,7},{7,8},{8,9},{9,10},{10,1... | collective-permute-start | bytes 24584 | tf_op jit(solution)/shard_map/ppermute | solution.py:546
  121.6 2.4 copy-start.6
  122.0 2.0 copy-start
  163.1 1.7 copy-start.2
  163.1 1.7 copy-start.7
  164.9 2.4 copy-start.42
  164.9 2.4 copy-start.12
  167.3 2.8 copy-start.10
  170.2 3.8 %copy-start.1 = (f32[2,128,1024]{2,1,0:T(8,128)S(1)}, f32[2,128,1024]{2,1,0:T(8,128)}, u32[]{:S(2)}) copy-start(f32[2,128,1024]{2,1,0:T(8,128)} %copy-done) | copy-start | bytes 3145732
  172.3 1.9 copy-start.22
  172.3 6.1 %collective-permute-start.1 = (bf16[2,2,1024]{2,1,0:T(2,128)(2,1)S(1)}, bf16[2,2,1024]{2,1,0:T(2,128)(2,1)S(1)}, u32[]{:S(2)}, u32[]{:S(2)}) collective-permute-start(bf16[2,2,1024]{2,1,0:T(2,128)(2,1)S(1)} %slice.87), channel_id=1, source_target_pairs={{1,0},{2,1},{3,2},{4,3},{5,4},{6,5},{7,6},{8,7},{9,8},{10,9},{11,1... | collective-permute-start | bytes 24584 | tf_op jit(solution)/shard_map/ppermute | solution.py:546
  307.3 1.5 copy-start.40
  307.3 2.3 copy-start.37
  308.8 2.3 copy-start.36
  312.4 3.9 %copy-start.3 = (f32[256,1024]{1,0:T(8,128)S(1)}, f32[256,1024]{1,0:T(8,128)}, u32[]{:S(2)}) copy-start(f32[256,1024]{1,0:T(8,128)} %get-tuple-element.44) | copy-start | bytes 3145732
  312.4 4.0 %copy-start.8 = (bf16[2,128,1024]{2,1,0:T(8,128)(2,1)S(1)}, bf16[2,128,1024]{2,1,0:T(8,128)(2,1)}, u32[]{:S(2)}) copy-start(bf16[2,128,1024]{2,1,0:T(8,128)(2,1)} %param.21) | copy-start | bytes 1572868
  314.6 1.7 copy-start.24
  314.6 1.7 copy-start.25
  314.6 1.7 copy-start.43
  314.6 1.7 copy-start.45
  314.6 1.7 copy-start.46
  316.4 1.8 copy-start.23
  316.4 1.8 copy-start.34
  316.4 1.8 copy-start.35
  316.4 3.1 copy-start.39
  318.2 1.3 copy-start.32
  318.2 1.3 copy-start.33
  318.2 2.1 copy-start.14
  318.2 2.1 copy-start.19
  318.3 2.1 copy-start.26
  318.3 2.2 copy-start.27
  320.4 1.5 copy-start.16
  320.4 1.5 copy-start.20
  320.4 2.1 copy-start.28
  320.4 2.2 copy-start.29
  322.7 1.5 copy-start.18
  322.7 1.6 copy-start.30
  322.7 2.1 copy-start.31
  324.2 2.1 copy-start.47
  324.2 2.1 copy-start.48
  (3 other events, 3.4 us)
